TPU v7x, 512 devices: a whole 4x8x8 slice. The times are simulated.
512 devices in a mesh: dp: 16 (over z, core), expert: 32 (over y, x).
Axes of the slice: x: 4, y: 8, z: 8, core: 2. Of those that a mesh axis runs over, the one named last changes fastest.
Arguments:
- tokens: bfloat16 [16384, 4096], P('expert', 'dp'), may hold values from -6 to 6
- cotangent: bfloat16 [16384, 4096], P('expert', 'dp'), may hold values from -6 to 6
- route: int32 [16384, 8], P('expert'), may hold values from 0 to 255, all different within a row
- prob: float32 [16384, 8], P('expert'), may hold values from 0.05 to 0.5
- quota: int32 [32], replicated, may hold values from 8 to 24, as said below
- w_gate: bfloat16 [32, 4096, 1024], P('expert', 'dp'), may hold values from -0.09375 to 0.09375
- w_up: bfloat16 [32, 4096, 1024], P('expert', 'dp'), may hold values from -0.09375 to 0.09375
- w_down: bfloat16 [32, 1024, 4096], P('expert', None, 'dp'), may hold values from -0.1875 to 0.1875
Outputs:
- mixed: bfloat16 [16384, 4096], P('expert', 'dp')
- grad_tokens: bfloat16 [16384, 4096], P('expert', 'dp')
- grad_gate: bfloat16 [32, 4096, 1024], P('expert', 'dp')
- grad_up: bfloat16 [32, 4096, 1024], P('expert', 'dp')
- grad_down: bfloat16 [32, 1024, 4096], P('expert', None, 'dp')
Inputs may be any that keep to these rules, and one draw needn't show every extreme that they name: `route`: each row names 8 different experts. quota[e] + quota[e + 16] = 32 for every e below 16.
All inputs are finite; a program needn't handle non-finite values.
Results may differ from a plain program's by a relative error of at most 0.035.
Values may be sent and summed in bfloat16 or wider, within the bound.
A program may use at most 64 MiB of HBM per device.

v0:
```python
import jax
import jax.numpy as jnp
from jax import lax
from jax.sharding import PartitionSpec as P

QHI = 24


contract_rows = (((0,), (0,)), ((), ()))
contract_cols = (((1,), (1,)), ((), ()))


def local(tokens, cotangent, route, prob, quota, w_gate, w_up, w_down):
    window = lax.axis_size("expert")
    tok_rows = tokens.shape[0]
    block_width = tokens.shape[1]
    expert_ids = jnp.arange(window, dtype=jnp.int32)
    matches = (route[:, :, None] == expert_ids).astype(jnp.int32)
    per_token = jnp.sum(matches, axis=1)
    before = jnp.cumsum(per_token, axis=0) - per_token
    position = jnp.sum(matches * before[:, None, :], axis=2)
    in_window = route < window
    quota_row = jnp.sum(matches * quota[None, None, :], axis=2)
    served = in_window & (position < quota_row)
    safe_route = jnp.where(in_window, route, 0)
    slot_count = QHI
    row_count = slot_count * window
    flat_index = position * window + safe_route
    slot_ids = jnp.arange(row_count, dtype=jnp.int32)
    picker = jnp.zeros((tok_rows, row_count), jnp.float32)
    weighted = jnp.zeros((tok_rows, row_count), jnp.float32)
    for pick_no in range(route.shape[1]):
        hit = ((flat_index[:, pick_no, None] == slot_ids) & served[:, pick_no, None]).astype(
            jnp.float32
        )
        picker = picker + hit
        weighted = weighted + hit * prob[:, pick_no, None]
    send_rows = lax.dot_general(
        picker.astype(jnp.bfloat16), tokens, contract_rows, preferred_element_type=jnp.float32
    )
    send_grads = lax.dot_general(
        weighted, cotangent.astype(jnp.float32), contract_rows, precision=lax.Precision.HIGHEST
    )
    shaped = (slot_count, window, block_width)
    recv_rows, recv_grads = (
        lax.all_to_all(
            send_rows.astype(jnp.bfloat16).reshape(shaped),
            "expert",
            split_axis=1,
            concat_axis=1,
            tiled=True,
        ),
        lax.all_to_all(
            send_grads.astype(jnp.bfloat16).reshape(shaped),
            "expert",
            split_axis=1,
            concat_axis=1,
            tiled=True,
        ),
    )
    slot_rows = recv_rows.reshape(row_count, block_width)
    slot_grads = recv_grads.reshape(row_count, block_width)
    gate_own = w_gate[0]
    up_own = w_up[0]
    down_own = w_down[0]
    gate_part = jnp.dot(slot_rows, gate_own, preferred_element_type=jnp.float32)
    up_part = jnp.dot(slot_rows, up_own, preferred_element_type=jnp.float32)
    back_part = lax.dot_general(
        slot_grads, down_own, contract_cols, preferred_element_type=jnp.float32
    )
    gate_pre, up_pre, back_hidden = (
        lax.psum(gate_part.astype(jnp.bfloat16), "dp").astype(jnp.float32),
        lax.psum(up_part.astype(jnp.bfloat16), "dp").astype(jnp.float32),
        lax.psum(back_part.astype(jnp.bfloat16), "dp").astype(jnp.float32),
    )
    sigmoid_g = jax.nn.sigmoid(gate_pre)
    active = gate_pre * sigmoid_g
    hidden = (active * up_pre).astype(jnp.bfloat16)
    grad_pre = (back_hidden * up_pre * sigmoid_g * (1.0 + gate_pre * (1.0 - sigmoid_g))).astype(
        jnp.bfloat16
    )
    grad_up_pre = (back_hidden * active).astype(jnp.bfloat16)
    out_rows = jnp.dot(hidden, down_own, preferred_element_type=jnp.float32)
    back_rows = lax.dot_general(
        grad_pre, gate_own, contract_cols, preferred_element_type=jnp.float32
    )
    back_rows = back_rows + lax.dot_general(
        grad_up_pre, up_own, contract_cols, preferred_element_type=jnp.float32
    )
    grad_gate = lax.dot_general(
        slot_rows, grad_pre, contract_rows, preferred_element_type=jnp.float32
    )
    grad_up = lax.dot_general(
        slot_rows, grad_up_pre, contract_rows, preferred_element_type=jnp.float32
    )
    grad_down = lax.dot_general(
        hidden, slot_grads, contract_rows, preferred_element_type=jnp.float32
    )
    out_send = out_rows.astype(jnp.bfloat16).reshape(shaped)
    back_send = back_rows.astype(jnp.bfloat16).reshape(shaped)
    back_out, back_grad = (
        lax.all_to_all(out_send, "expert", split_axis=1, concat_axis=1, tiled=True),
        lax.all_to_all(back_send, "expert", split_axis=1, concat_axis=1, tiled=True),
    )
    mixed = jnp.dot(
        weighted,
        back_out.reshape(row_count, block_width).astype(jnp.float32),
        precision=lax.Precision.HIGHEST,
    )
    grad_tokens = jnp.dot(
        picker.astype(jnp.bfloat16),
        back_grad.reshape(row_count, block_width),
        preferred_element_type=jnp.float32,
    )
    return (
        mixed.astype(jnp.bfloat16),
        grad_tokens.astype(jnp.bfloat16),
        grad_gate.astype(jnp.bfloat16)[None],
        grad_up.astype(jnp.bfloat16)[None],
        grad_down.astype(jnp.bfloat16)[None],
    )


def solution(mesh):
    placed = (
        P("expert", "dp"),
        P("expert", "dp"),
        P("expert", None),
        P("expert", None),
        P(),
        P("expert", "dp", None),
        P("expert", "dp", None),
        P("expert", None, "dp"),
    )
    return jax.shard_map(
        local,
        mesh=mesh,
        in_specs=placed,
        out_specs=(
            P("expert", "dp"),
            P("expert", "dp"),
            P("expert", "dp", None),
            P("expert", "dp", None),
            P("expert", None, "dp"),
        ),
        check_vma=False,
    )
```

profile of v0, /device:TPU:8, one launch (start us, length us, event | category | flops | bytes accessed | tf_op | source)
XLA Modules:
  0.0 254.1 jit_solution(12869343322832261600)
XLA Ops:
  7.2 0.0 copy-start
  7.2 0.8 convert_reduce_fusion
  8.0 1.2 reduce-window.6
  9.2 0.2 slice_reduce_fusion
  9.5 0.1 fusion.28
  9.6 0.9 select_reduce_fusion
  10.5 0.7 fusion.29
  11.2 0.7 compare_and_fusion
  12.0 0.1 slice_reduce_fusion.8
  12.1 3.8 %convolution_convert_fusion.8 = bf16[768,256]{1,0:T(8,128)(2,1)S(1)} fusion(bf16[512,256]{1,0:T(8,128)(2,1)} %param.8, s32[512]{0:T(512)S(1)} %bitcast.94, s32[512]{0:T(512)S(1)} %bitcast.98, s32[512]{0:T(512)S(1)} %bitcast.102, s32[512]{0:T(512)S(1)} %bitcast.106, s32[512]{0:T(512)S(1)} %bitcast.110, s32[512]{0:T(512)S(1)} %bitcast.114, ...), kind=kOutput, calls=%fused_computation.43 | convolution fusion | flops 214106112 | bytes 675840 | tf_op jit(solution)/shard_map/dot_general | solution.py:38
  15.9 0.0 copy-start.8
  15.9 0.0 copy-start.49
  16.0 1.0 copy.40
  16.9 10.2 %all-to-all-start = ((bf16[24,32,256]{2,0,1:T(8,128)(2,1)}), bf16[24,32,256]{2,0,1:T(8,128)(2,1)S(1)}, u32[]{:S(2)}, u32[]{:S(2)}) async-start(bf16[24,32,256]{2,0,1:T(8,128)(2,1)} %copy.40), calls=%async_computation | async-start | bytes 786432 | tf_op jit(solution)/shard_map/all_to_all | solution.py:46
  27.1 0.0 copy-done.8
  27.2 0.0 copy-start.29
  27.2 0.0 copy-start.31
  27.2 0.0 copy-done.9
  27.2 0.0 copy-done.11
  27.2 0.0 copy-done.13
  27.2 0.0 copy-done.15
  27.2 0.0 copy-done.33
  27.3 0.0 copy-done.35
  27.3 0.3 copy-done.17
  27.6 0.1 copy-done.19
  27.7 0.0 copy-done.25
  27.8 0.0 copy-done.27
  27.8 0.0 copy-done.31
  27.8 4.5 %convolution_convert_fusion.6 = bf16[768,256]{1,0:T(8,128)(2,1)S(1)} fusion(bf16[512,256]{1,0:T(8,128)(2,1)S(1)} %copy-done.49, f32[512]{0:T(512)S(1)} %bitcast.134, s32[512]{0:T(512)S(1)} %bitcast.95, f32[512]{0:T(512)S(1)} %bitcast.136, s32[512]{0:T(512)S(1)} %bitcast.99, f32[512]{0:T(512)S(1)} %bitcast.124, s32[512]{0:T(512)S(1)} %bitcast.103, ...), kind=kOutput, calls=%fused_computation.40 | convolution fusion | flops 1220345856 | bytes 692224 | tf_op jit(solution)/shard_map/dot_general | solution.py:41
  32.3 0.0 copy-start.2
  32.3 1.0 copy.44
  33.2 8.6 %all-to-all-done = bf16[24,32,256]{2,0,1:T(8,128)(2,1)S(1)} async-done(((bf16[24,32,256]{2,0,1:T(8,128)(2,1)}), bf16[24,32,256]{2,0,1:T(8,128)(2,1)S(1)}, u32[]{:S(2)}, u32[]{:S(2)}) %all-to-all-start) | async-done | bytes 393248 | tf_op jit(solution)/shard_map/all_to_all | solution.py:46
  41.8 4.9 %all-to-all-start.2 = ((bf16[24,32,256]{2,0,1:T(8,128)(2,1)}), bf16[24,32,256]{2,0,1:T(8,128)(2,1)S(1)}, u32[]{:S(2)}, u32[]{:S(2)}) async-start(bf16[24,32,256]{2,0,1:T(8,128)(2,1)} %copy.44), calls=%async_computation.2 | async-start | bytes 786432 | tf_op jit(solution)/shard_map/all_to_all | solution.py:53
  46.7 0.0 copy-start.3
  46.7 0.2 all-reduce.3.cloned.1.call-start
  46.9 0.1 copy.41
  47.0 1.8 convolution_convert_fusion.1
  48.8 1.7 convolution_convert_fusion.2
  50.5 10.1 %all-to-all-done.2 = bf16[24,32,256]{2,0,1:T(8,128)(2,1)S(1)} async-done(((bf16[24,32,256]{2,0,1:T(8,128)(2,1)}), bf16[24,32,256]{2,0,1:T(8,128)(2,1)S(1)}, u32[]{:S(2)}, u32[]{:S(2)}) %all-to-all-start.2) | async-done | bytes 393248 | tf_op jit(solution)/shard_map/all_to_all | solution.py:53
  60.6 0.1 copy.45
  60.7 0.8 copy-done.6
  61.5 1.9 convolution_convert_fusion
  63.3 0.0 all-reduce.3.cloned.1.call-update
  63.3 129.3 %all-reduce.3.cloned.1.call-done = (bf16[768,1024]{1,0:T(8,128)(2,1)}, bf16[768,1024]{1,0:T(8,128)(2,1)}, bf16[768,1024]{1,0:T(8,128)(2,1)}) async-done(((bf16[768,1024]{1,0:T(8,128)(2,1)}, bf16[768,1024]{1,0:T(8,128)(2,1)}, bf16[768,1024]{1,0:T(8,128)(2,1)}), (bf16[768,1024]{1,0:T(8,128)(2,1)}, bf16[768,1024]{1,0:T(8,128)(2,1)}, bf16[768,1024]{1,0:T(8,128)(2,1)})) %all-reduce.3.cloned.1.call-update) | async-done | bytes 4718608 | tf_op jit(solution)/shard_map/psum | solution.py:73
  192.6 4.6 %fusion.4 = (bf16[768,1024]{1,0:T(8,128)(2,1)S(1)}, bf16[768,1024]{1,0:T(8,128)(2,1)}, bf16[768,1024]{1,0:T(8,128)(2,1)S(1)}) fusion(bf16[768,1024]{1,0:T(8,128)(2,1)} %get-tuple-element.17, bf16[768,1024]{1,0:T(8,128)(2,1)} %get-tuple-element.16, bf16[768,1024]{1,0:T(8,128)(2,1)} %get-tuple-element.15), kind=kLoop, calls=%fused_computation.10 | loop fusion | flops 14155776 | bytes 9437184 | tf_op jit(solution)/shard_map/convert_element_type | solution.py:82
  197.2 1.2 copy-done.4
  198.4 0.6 convolution_convert_fusion.7
  198.9 1.0 copy.42
  199.9 9.9 %all-to-all-start.1 = ((bf16[24,32,256]{2,0,1:T(8,128)(2,1)}), bf16[24,32,256]{2,0,1:T(8,128)(2,1)}, u32[]{:S(2)}, u32[]{:S(2)}) async-start(bf16[24,32,256]{2,0,1:T(8,128)(2,1)} %copy.42), calls=%async_computation.1 | async-start | bytes 786432 | tf_op jit(solution)/shard_map/all_to_all | solution.py:102
  209.8 2.0 fusion.25
  211.8 0.6 fusion.17
  212.5 1.0 copy.46
  213.5 1.4 fusion.19
  214.9 1.4 fusion.18
  216.3 7.4 %all-to-all-done.1 = bf16[24,32,256]{2,0,1:T(8,128)(2,1)} async-done(((bf16[24,32,256]{2,0,1:T(8,128)(2,1)}), bf16[24,32,256]{2,0,1:T(8,128)(2,1)}, u32[]{:S(2)}, u32[]{:S(2)}) %all-to-all-start.1) | async-done | bytes 393248 | tf_op jit(solution)/shard_map/all_to_all | solution.py:102
  223.7 4.9 %all-to-all-start.3 = ((bf16[24,32,256]{2,0,1:T(8,128)(2,1)}), bf16[24,32,256]{2,0,1:T(8,128)(2,1)S(1)}, u32[]{:S(2)}, u32[]{:S(2)}) async-start(bf16[24,32,256]{2,0,1:T(8,128)(2,1)} %copy.46), calls=%async_computation.3 | async-start | bytes 786432 | tf_op jit(solution)/shard_map/all_to_all | solution.py:103
  228.7 0.0 copy-start.30
  228.7 0.0 copy-start.32
  228.8 1.4 fusion.20
  230.2 1.1 copy.43
  231.5 6.8 %convolution_convert_fusion.9 = bf16[512,256]{1,0:T(8,128)(2,1)} fusion(bf16[768,256]{1,0:T(8,128)(2,1)S(1)} %bitcast.86, f32[512]{0:T(512)S(1)} %bitcast.135, s32[512]{0:T(512)S(1)} %bitcast.96, f32[512]{0:T(512)S(1)} %bitcast.137, s32[512]{0:T(512)S(1)} %bitcast.100, f32[512]{0:T(512)S(1)} %bitcast.125, s32[512]{0:T(512)S(1)} %bitcast.104, ...), kind=kOutput, calls=%fused_computation.47 | convolution fusion | flops 1220280320 | bytes 692224 | tf_op jit(solution)/shard_map/dot_general | solution.py:105
  238.3 3.8 %all-to-all-done.3 = bf16[24,32,256]{2,0,1:T(8,128)(2,1)S(1)} async-done(((bf16[24,32,256]{2,0,1:T(8,128)(2,1)}), bf16[24,32,256]{2,0,1:T(8,128)(2,1)S(1)}, u32[]{:S(2)}, u32[]{:S(2)}) %all-to-all-start.3) | async-done | bytes 393248 | tf_op jit(solution)/shard_map/all_to_all | solution.py:103
  242.1 0.1 copy.47
  242.2 5.1 %convolution_convert_fusion.10 = bf16[512,256]{1,0:T(8,128)(2,1)} fusion(bf16[768,256]{1,0:T(8,128)(2,1)S(1)} %bitcast.85, s32[512]{0:T(512)S(1)} %bitcast.97, s32[512]{0:T(512)S(1)} %bitcast.101, s32[512]{0:T(512)S(1)} %bitcast.105, s32[512]{0:T(512)S(1)} %bitcast.109, s32[512]{0:T(512)S(1)} %bitcast.113, s32[512]{0:T(512)S(1)} %bitcast.117, ...), kind=kOutput, calls=%fused_computation.48 | convolution fusion | flops 214040576 | bytes 675840 | tf_op jit(solution)/shard_map/dot_general | solution.py:110
  (82 shorter events, 0.2 us)
Async XLA Ops:
  7.2 54.3 %copy-start = (bf16[1,1024,256]{2,1,0:T(8,128)(2,1)S(1)}, bf16[1,1024,256]{2,1,0:T(8,128)(2,1)}, u32[]{:S(2)}) copy-start(bf16[1,1024,256]{2,1,0:T(8,128)(2,1)} %param.15) | copy-start | bytes 1572868
  12.0 15.2 %copy-start.9 = (s32[512,1]{0,1:T(1,128)}, s32[512,1]{0,1:T(1,128)S(1)}, u32[]{:S(2)}) copy-start(s32[512,1]{0,1:T(1,128)S(1)} %get-tuple-element.33) | copy-start | bytes 6148
  12.0 15.2 %copy-start.11 = (s32[512,1]{0,1:T(1,128)}, s32[512,1]{0,1:T(1,128)S(1)}, u32[]{:S(2)}) copy-start(s32[512,1]{0,1:T(1,128)S(1)} %get-tuple-element.34) | copy-start | bytes 6148
  12.0 15.2 %copy-start.13 = (s32[512,1]{0,1:T(1,128)}, s32[512,1]{0,1:T(1,128)S(1)}, u32[]{:S(2)}) copy-start(s32[512,1]{0,1:T(1,128)S(1)} %get-tuple-element.35) | copy-start | bytes 6148
  12.0 15.2 %copy-start.15 = (s32[512,1]{0,1:T(1,128)}, s32[512,1]{0,1:T(1,128)S(1)}, u32[]{:S(2)}) copy-start(s32[512,1]{0,1:T(1,128)S(1)} %get-tuple-element.36) | copy-start | bytes 6148
  12.1 15.2 %copy-start.33 = (pred[512]{0:T(512)(128)(4,1)}, pred[512]{0:T(512)(128)(4,1)S(1)}, u32[]{:S(2)}) copy-start(pred[512]{0:T(512)(128)(4,1)S(1)} %get-tuple-element.7) | copy-start | bytes 1540
  12.1 15.2 %copy-start.35 = (pred[512]{0:T(512)(128)(4,1)}, pred[512]{0:T(512)(128)(4,1)S(1)}, u32[]{:S(2)}) copy-start(pred[512]{0:T(512)(128)(4,1)S(1)} %get-tuple-element.8) | copy-start | bytes 1540
  12.1 15.2 %copy-start.37 = (pred[512]{0:T(512)(128)(4,1)}, pred[512]{0:T(512)(128)(4,1)S(1)}, u32[]{:S(2)}) copy-start(pred[512]{0:T(512)(128)(4,1)S(1)} %get-tuple-element.9) | copy-start | bytes 1540
  12.1 15.2 %copy-start.39 = (pred[512]{0:T(512)(128)(4,1)}, pred[512]{0:T(512)(128)(4,1)S(1)}, u32[]{:S(2)}) copy-start(pred[512]{0:T(512)(128)(4,1)S(1)} %get-tuple-element.10) | copy-start | bytes 1540
  12.1 15.2 %copy-start.41 = (pred[512]{0:T(512)(128)(4,1)}, pred[512]{0:T(512)(128)(4,1)S(1)}, u32[]{:S(2)}) copy-start(pred[512]{0:T(512)(128)(4,1)S(1)} %get-tuple-element.11) | copy-start | bytes 1540
  12.1 15.2 %copy-start.43 = (pred[512]{0:T(512)(128)(4,1)}, pred[512]{0:T(512)(128)(4,1)S(1)}, u32[]{:S(2)}) copy-start(pred[512]{0:T(512)(128)(4,1)S(1)} %get-tuple-element.12) | copy-start | bytes 1540
  12.1 15.2 %copy-start.45 = (pred[512]{0:T(512)(128)(4,1)}, pred[512]{0:T(512)(128)(4,1)S(1)}, u32[]{:S(2)}) copy-start(pred[512]{0:T(512)(128)(4,1)S(1)} %get-tuple-element.13) | copy-start | bytes 1540
  12.1 15.2 %copy-start.47 = (pred[512]{0:T(512)(128)(4,1)}, pred[512]{0:T(512)(128)(4,1)S(1)}, u32[]{:S(2)}) copy-start(pred[512]{0:T(512)(128)(4,1)S(1)} %get-tuple-element.14) | copy-start | bytes 1540
  15.9 11.2 %copy-start.8 = (f32[512,8]{0,1:T(8,128)S(1)}, f32[512,8]{0,1:T(8,128)}, u32[]{:S(2)}) copy-start(f32[512,8]{0,1:T(8,128)} %param.11) | copy-start | bytes 49156
  15.9 11.8 %copy-start.49 = (bf16[512,256]{1,0:T(8,128)(2,1)S(1)}, bf16[512,256]{1,0:T(8,128)(2,1)}, u32[]{:S(2)}) copy-start(bf16[512,256]{1,0:T(8,128)(2,1)} %param.9) | copy-start | bytes 786436
  16.9 24.9 %all-to-all-start = ((bf16[24,32,256]{2,0,1:T(8,128)(2,1)}), bf16[24,32,256]{2,0,1:T(8,128)(2,1)S(1)}, u32[]{:S(2)}, u32[]{:S(2)}) async-start(bf16[24,32,256]{2,0,1:T(8,128)(2,1)} %copy.40), calls=%async_computation | async-start | bytes 786432 | tf_op jit(solution)/shard_map/all_to_all | solution.py:46
  27.1 0.5 copy-start.17
  27.1 0.6 copy-start.19
  27.1 0.6 copy-start.21
  27.2 0.6 copy-start.23
  27.2 0.6 copy-start.25
  27.2 0.6 copy-start.27
  27.2 0.6 copy-start.29
  27.2 0.6 copy-start.31
  32.3 14.8 %copy-start.2 = (bf16[1,256,1024]{2,1,0:T(8,128)(2,1)S(1)}, bf16[1,256,1024]{2,1,0:T(8,128)(2,1)}, u32[]{:S(2)}) copy-start(bf16[1,256,1024]{2,1,0:T(8,128)(2,1)} %param.14) | copy-start | bytes 1572868
  41.8 18.8 %all-to-all-start.2 = ((bf16[24,32,256]{2,0,1:T(8,128)(2,1)}), bf16[24,32,256]{2,0,1:T(8,128)(2,1)S(1)}, u32[]{:S(2)}, u32[]{:S(2)}) async-start(bf16[24,32,256]{2,0,1:T(8,128)(2,1)} %copy.44), calls=%async_computation.2 | async-start | bytes 786432 | tf_op jit(solution)/shard_map/all_to_all | solution.py:53
  46.7 2.1 copy-start.3
  46.7 145.9 %all-reduce.3.cloned.1.call-start = ((), (), s32[]{:S(2)}) async-start(), calls=%async_computation.4 | async-start | bytes 9437184 | tf_op jit(solution)/shard_map/psum | solution.py:73
  60.7 0.8 copy-start.6
  197.2 1.2 copy-start.4
  199.9 23.8 %all-to-all-start.1 = ((bf16[24,32,256]{2,0,1:T(8,128)(2,1)}), bf16[24,32,256]{2,0,1:T(8,128)(2,1)}, u32[]{:S(2)}, u32[]{:S(2)}) async-start(bf16[24,32,256]{2,0,1:T(8,128)(2,1)} %copy.42), calls=%async_computation.1 | async-start | bytes 786432 | tf_op jit(solution)/shard_map/all_to_all | solution.py:102
  212.4 2.4 copy-start.1
  214.8 13.7 %copy-start.5 = (bf16[768,1024]{1,0:T(8,128)(2,1)S(1)}, bf16[768,1024]{1,0:T(8,128)(2,1)}, u32[]{:S(2)}) copy-start(bf16[768,1024]{1,0:T(8,128)(2,1)} %copy-done.4) | copy-start | bytes 4718596
  214.9 13.7 %copy-start.7 = (bf16[24,32,256]{2,1,0:T(8,128)(2,1)S(1)}, bf16[24,32,256]{2,1,0:T(8,128)(2,1)}, u32[]{:S(2)}) copy-start(bf16[24,32,256]{2,1,0:T(8,128)(2,1)} %copy-done.6) | copy-start | bytes 1179652
  223.7 18.4 %all-to-all-start.3 = ((bf16[24,32,256]{2,0,1:T(8,128)(2,1)}), bf16[24,32,256]{2,0,1:T(8,128)(2,1)S(1)}, u32[]{:S(2)}, u32[]{:S(2)}) async-start(bf16[24,32,256]{2,0,1:T(8,128)(2,1)} %copy.46), calls=%async_computation.3 | async-start | bytes 786432 | tf_op jit(solution)/shard_map/all_to_all | solution.py:103
  228.6 2.7 %copy-start.10 = (s32[512,1]{0,1:T(1,128)S(1)}, s32[512,1]{0,1:T(1,128)}, u32[]{:S(2)}) copy-start(s32[512,1]{0,1:T(1,128)} %copy-done.9) | copy-start | bytes 6148
  228.6 2.7 %copy-start.12 = (s32[512,1]{0,1:T(1,128)S(1)}, s32[512,1]{0,1:T(1,128)}, u32[]{:S(2)}) copy-start(s32[512,1]{0,1:T(1,128)} %copy-done.11) | copy-start | bytes 6148
  228.6 2.7 %copy-start.14 = (s32[512,1]{0,1:T(1,128)S(1)}, s32[512,1]{0,1:T(1,128)}, u32[]{:S(2)}) copy-start(s32[512,1]{0,1:T(1,128)} %copy-done.13) | copy-start | bytes 6148
  228.6 2.7 %copy-start.16 = (s32[512,1]{0,1:T(1,128)S(1)}, s32[512,1]{0,1:T(1,128)}, u32[]{:S(2)}) copy-start(s32[512,1]{0,1:T(1,128)} %copy-done.15) | copy-start | bytes 6148
  228.6 2.7 %copy-start.18 = (f32[512,1]{0,1:T(1,128)S(1)}, f32[512,1]{0,1:T(1,128)}, u32[]{:S(2)}) copy-start(f32[512,1]{0,1:T(1,128)} %copy-done.17) | copy-start | bytes 6148
  228.6 2.7 %copy-start.20 = (f32[512,1]{0,1:T(1,128)S(1)}, f32[512,1]{0,1:T(1,128)}, u32[]{:S(2)}) copy-start(f32[512,1]{0,1:T(1,128)} %copy-done.19) | copy-start | bytes 6148
  228.6 2.7 %copy-start.22 = (f32[512,1]{0,1:T(1,128)S(1)}, f32[512,1]{0,1:T(1,128)}, u32[]{:S(2)}) copy-start(f32[512,1]{0,1:T(1,128)} %copy-done.21) | copy-start | bytes 6148
  228.6 2.7 %copy-start.24 = (f32[512,1]{0,1:T(1,128)S(1)}, f32[512,1]{0,1:T(1,128)}, u32[]{:S(2)}) copy-start(f32[512,1]{0,1:T(1,128)} %copy-done.23) | copy-start | bytes 6148
  228.7 2.7 %copy-start.26 = (f32[512,1]{0,1:T(1,128)S(1)}, f32[512,1]{0,1:T(1,128)}, u32[]{:S(2)}) copy-start(f32[512,1]{0,1:T(1,128)} %copy-done.25) | copy-start | bytes 6148
  228.7 2.7 %copy-start.28 = (f32[512,1]{0,1:T(1,128)S(1)}, f32[512,1]{0,1:T(1,128)}, u32[]{:S(2)}) copy-start(f32[512,1]{0,1:T(1,128)} %copy-done.27) | copy-start | bytes 6148
  228.7 2.7 %copy-start.30 = (f32[512,1]{0,1:T(1,128)S(1)}, f32[512,1]{0,1:T(1,128)}, u32[]{:S(2)}) copy-start(f32[512,1]{0,1:T(1,128)} %copy-done.29) | copy-start | bytes 6148
  228.7 2.7 %copy-start.32 = (f32[512,1]{0,1:T(1,128)S(1)}, f32[512,1]{0,1:T(1,128)}, u32[]{:S(2)}) copy-start(f32[512,1]{0,1:T(1,128)} %copy-done.31) | copy-start | bytes 6148
  228.7 2.7 %copy-start.34 = (pred[512]{0:T(512)(128)(4,1)S(1)}, pred[512]{0:T(512)(128)(4,1)}, u32[]{:S(2)}) copy-start(pred[512]{0:T(512)(128)(4,1)} %copy-done.33) | copy-start | bytes 1540
  228.7 2.7 %copy-start.36 = (pred[512]{0:T(512)(128)(4,1)S(1)}, pred[512]{0:T(512)(128)(4,1)}, u32[]{:S(2)}) copy-start(pred[512]{0:T(512)(128)(4,1)} %copy-done.35) | copy-start | bytes 1540
  228.7 2.7 %copy-start.38 = (pred[512]{0:T(512)(128)(4,1)S(1)}, pred[512]{0:T(512)(128)(4,1)}, u32[]{:S(2)}) copy-start(pred[512]{0:T(512)(128)(4,1)} %copy-done.37) | copy-start | bytes 1540
  228.7 2.7 %copy-start.40 = (pred[512]{0:T(512)(128)(4,1)S(1)}, pred[512]{0:T(512)(128)(4,1)}, u32[]{:S(2)}) copy-start(pred[512]{0:T(512)(128)(4,1)} %copy-done.39) | copy-start | bytes 1540
  228.7 2.7 %copy-start.42 = (pred[512]{0:T(512)(128)(4,1)S(1)}, pred[512]{0:T(512)(128)(4,1)}, u32[]{:S(2)}) copy-start(pred[512]{0:T(512)(128)(4,1)} %copy-done.41) | copy-start | bytes 1540
  228.8 2.7 %copy-start.44 = (pred[512]{0:T(512)(128)(4,1)S(1)}, pred[512]{0:T(512)(128)(4,1)}, u32[]{:S(2)}) copy-start(pred[512]{0:T(512)(128)(4,1)} %copy-done.43) | copy-start | bytes 1540
  228.8 2.7 %copy-start.46 = (pred[512]{0:T(512)(128)(4,1)S(1)}, pred[512]{0:T(512)(128)(4,1)}, u32[]{:S(2)}) copy-start(pred[512]{0:T(512)(128)(4,1)} %copy-done.45) | copy-start | bytes 1540
  228.8 2.7 %copy-start.48 = (pred[512]{0:T(512)(128)(4,1)S(1)}, pred[512]{0:T(512)(128)(4,1)}, u32[]{:S(2)}) copy-start(pred[512]{0:T(512)(128)(4,1)} %copy-done.47) | copy-start | bytes 1540
Sparse Core Ops, SparseCore 0:
  63.5 129.1 all-reduce.2
where the time goes:
time: 255 us; the launch traced here: 254 us
  waiting for transfers between devices  159 us (62%)
  matrix products  32.9 us (13%)
  starting transfers between devices  30 us (12%)
  between operations  14.8 us (6%)
  other arithmetic  9.07 us (4%)
  local copies, waits for them, and re-layouts  8.08 us (3%)
    psum x1, waiting for transfers between devices, local(): lax.psum(up_part.astype(jnp.bfloat16), 'dp').astype(jnp.float32)  129 us
    all_to_all x1, starting transfers between devices, local(): lax.all_to_all(send_rows.astype(jnp.bfloat16).reshape(shaped), 'expert',...  10.2 us
    all_to_all x1, waiting for transfers between devices, local(): lax.all_to_all(send_grads.astype(jnp.bfloat16).reshape(shaped), 'expert',...  10.1 us
    all_to_all x1, starting transfers between devices, local(): lax.all_to_all(out_send, 'expert', split_axis=1, concat_axis=1, tiled=True)  9.9 us
    all_to_all x1, waiting for transfers between devices, local(): lax.all_to_all(send_rows.astype(jnp.bfloat16).reshape(shaped), 'expert',...  8.57 us
    all_to_all x1, waiting for transfers between devices, local(): lax.all_to_all(out_send, 'expert', split_axis=1, concat_axis=1, tiled=True)  7.42 us
    dot_general x1, matrix products, local(): jnp.dot(weighted, back_out.reshape(row_count, block_width).astype(jnp.flo...  6.84 us
  transfers between devices with their start and end apart: 5, of which 5 were waited for; matrix products, arithmetic and copies ran while one was open for 10% of the time, Pallas kernels for 0%

commit v1 on v0

v1 whole, which is shorter than its diff:
```python
import functools

import jax
import jax.numpy as jnp
from jax import lax
from jax.experimental import pallas as pl
from jax.experimental.pallas import tpu as pltpu
from jax.sharding import PartitionSpec as P

QHI = 24
CH = 3
SL = QHI // CH
MESH = pl.DeviceIdType.MESH
F32 = jnp.float32
BF16 = jnp.bfloat16
ROWS = (((0,), (0,)), ((), ()))
COLS = (((1,), (1,)), ((), ()))


def dot(a, b, dims=(((1,), (0,)), ((), ()))):
    return lax.dot_general(a, b, dims, preferred_element_type=F32)


def kernel(
    n_exp, n_z,
    tokens, cot, route, prob, quota, wg_in, wu_in, wd_in,
    mixed, gtok, ggate, gup, gdown,
    wg, wu, wd, send, recv, trash, xs, gs, part, rsr, ag, outb, cbuf,
    wmat, gacc, gdacc, gsend, gdsend, grecv, gdrecv,
    w_loc, w_snd, w_rcv, d_snd, d_rcv, rs_snd, rs_rcv, ag_snd, ag_rcv,
    c_snd, c_rcv, g_snd, g_rcv,
):
    dp = lax.axis_index("dp")
    me = lax.axis_index("expert")
    z = dp // 2
    core = lax.rem(dp, 2)
    par = lax.rem(me, 2)
    n_src = n_exp // 2
    half = n_z // 2
    tok_n, feat = tokens.shape
    hid = wg.shape[1]
    hh = hid // 2
    rows = n_src * SL
    zr = rows // n_z
    lanes = 128

    def dev(e, zz, cc):
        return {"expert": e, "dp": zz * 2 + cc}

    right, left = lax.rem(z + 1, n_z), lax.rem(z + n_z - 1, n_z)

    barrier = pltpu.get_barrier_semaphore()

    def greet(e, zz, cc):
        pl.semaphore_signal(barrier, inc=1, device_id=dev(e, zz, cc), device_id_type=MESH)

    greet(me, right, core)
    greet(me, left, core)

    @pl.loop(0, n_exp)
    def _(t):
        e = lax.rem(me + t, n_exp)

        @pl.when(jnp.logical_or(t > 0, core != par))
        def _():
            greet(e, z, par)

    @pl.loop(0, n_src)
    def _(t):
        greet(2 * t + core, z, 1 - par)

    own = [
        pltpu.make_async_copy(wg_in.at[0], wg.at[pl.ds(core * feat, feat)], w_loc.at[0]),
        pltpu.make_async_copy(wu_in.at[0], wu.at[pl.ds(core * feat, feat)], w_loc.at[1]),
        pltpu.make_async_copy(wd_in.at[0], wd.at[core], w_loc.at[2]),
    ]
    for copy in own:
        copy.start()

    lane = lax.broadcasted_iota(jnp.int32, (tok_n, lanes), 1)
    match = jnp.zeros((tok_n, lanes), F32)
    pe = jnp.zeros((tok_n, lanes), F32)
    for k in range(route.shape[1]):
        hit = route[:, k : k + 1] == lane
        match = jnp.where(hit, 1.0, match)
        pe = jnp.where(hit, prob[:, k : k + 1], pe)
    lower = lax.broadcasted_iota(jnp.int32, (tok_n, tok_n), 1) < lax.broadcasted_iota(
        jnp.int32, (tok_n, tok_n), 0
    )
    before = dot(lower.astype(F32).astype(BF16), match.astype(BF16))
    lane1 = lax.broadcasted_iota(jnp.int32, (1, lanes), 1)
    quotas = jnp.zeros((1, lanes), jnp.int32)
    for e in range(n_exp):
        quotas = jnp.where(lane1 == e, quota[e], quotas)
    eff = jnp.where((match > 0.0) & (before < quotas.astype(F32)), before, 255.0)
    eff_t = eff.T[:n_exp]
    pe_t = pe.T[:n_exp]

    others = par == core
    pl.semaphore_wait(barrier, n_exp + n_src + 2 - others.astype(jnp.int32))

    shared = [
        (wg_in.at[0], wg.at[pl.ds(core * feat, feat)]),
        (wu_in.at[0], wu.at[pl.ds(core * feat, feat)]),
        (wd_in.at[0], wd.at[core]),
    ]

    def weight_copy(i):
        return pltpu.make_async_remote_copy(
            src_ref=shared[i][0], dst_ref=shared[i][1], send_sem=w_snd.at[i], recv_sem=w_rcv.at[i],
            device_id=dev(me, z, 1 - core), device_id_type=MESH,
        )

    slot = lax.broadcasted_iota(jnp.int32, (n_exp, SL, tok_n), 1).astype(F32)
    for c in range(CH):
        hit = eff_t[:, None, :] == slot + float(c * SL)
        pick = jnp.where(hit, 1.0, 0.0).reshape(n_exp * SL, tok_n)
        weight = jnp.where(hit, pe_t[:, None, :], 0.0).reshape(n_exp * SL, tok_n)
        slot_prob = jnp.sum(weight, axis=1, keepdims=True)
        pick = pick.astype(BF16)
        picked = dot(pick, tokens[...]).reshape(n_exp, SL, feat)
        grads = (dot(pick, cot[...]) * slot_prob).reshape(n_exp, SL, feat)
        send[c] = jnp.concatenate([picked, grads], axis=1).astype(BF16)

        @pl.loop(0, n_exp)
        def _(t):
            e = lax.rem(me + t + 1, n_exp)
            there = jnp.logical_or(e != me, core != par)

            @pl.when(there)
            def _():
                pltpu.make_async_remote_copy(
                    src_ref=send.at[c, e], dst_ref=recv.at[c, core, me // 2],
                    send_sem=d_snd.at[c], recv_sem=d_rcv.at[c],
                    device_id=dev(e, z, par), device_id_type=MESH,
                ).start()

            @pl.when(jnp.logical_not(there))
            def _():
                pltpu.make_async_copy(send.at[c, e], recv.at[c, core, me // 2], d_rcv.at[c]).start()
                pltpu.make_async_copy(send.at[c, e], trash.at[0, c], d_snd.at[c]).start()

        if c == 0:
            for i in range(3):
                weight_copy(i).start()

    wide = n_exp * 2 * SL
    spread = (
        lax.broadcasted_iota(jnp.int32, (lanes, wide), 1) // (2 * SL)
        == lax.broadcasted_iota(jnp.int32, (lanes, wide), 0)
    ).astype(F32).astype(BF16)
    eff_x = dot(eff.astype(BF16), spread)
    pe_hi = pe.astype(BF16)
    pe_lo = (pe - pe_hi.astype(F32)).astype(BF16)
    hi_x = dot(pe_hi, spread)
    lo_x = dot(pe_lo, spread)
    place = lax.rem(lax.broadcasted_iota(jnp.int32, (tok_n, wide), 1), 2 * SL)
    for c in range(CH):
        out_hit = eff_x == (place + c * SL).astype(F32)
        out_hit = out_hit & (place < SL)
        back_hit = (eff_x == (place + (c - 1) * SL).astype(F32)) & (place >= SL)
        wmat[c, 0] = jnp.where(out_hit, hi_x, 0.0).astype(BF16)
        wmat[c, 1] = jnp.where(out_hit, lo_x, 0.0).astype(BF16)
        wmat[c, 2] = jnp.where(back_hit, 1.0, 0.0).astype(BF16)

    for copy in own:
        copy.wait()
    for i in range(3):
        weight_copy(i).wait_recv()

    def rs_copy(c, way, step):
        k = half - step
        if way == 0:
            d, to = lax.rem(z + k, n_z), right
        else:
            d, to = lax.rem(z + n_z - k, n_z), left
        src, dst = part.at[c, d], rsr.at[c, way, step]
        if step == 0:
            src, dst = src.at[way], dst.at[way]
        return pltpu.make_async_remote_copy(
            src_ref=src, dst_ref=dst, send_sem=rs_snd.at[c, way, step], recv_sem=rs_rcv.at[c, way, step],
            device_id=dev(me, to, core), device_id_type=MESH,
        )

    def ag_copy(c, way, step):
        if way == 0:
            d, to = lax.rem(z + n_z - step, n_z), right
        else:
            d, to = lax.rem(z + step, n_z), left
        ref = ag.at[c, d]
        if step == half - 1:
            ref = ref.at[way]
        return pltpu.make_async_remote_copy(
            src_ref=ref, dst_ref=ref, send_sem=ag_snd.at[c, way, step], recv_sem=ag_rcv.at[c, way, step],
            device_id=dev(me, to, core), device_id_type=MESH,
        )

    def ag_landed(c, way, step):
        if way == 0:
            d = lax.rem(z + n_z - step - 1, n_z)
        else:
            d = lax.rem(z + step + 1, n_z)
        ref = ag.at[c, d]
        if step == half - 1:
            ref = ref.at[way]
        return pltpu.make_async_copy(ref, ref, ag_rcv.at[c, way, step])

    def rs_landed(c, way, step):
        ref = rsr.at[c, way, step]
        if step == 0:
            ref = ref.at[way]
        return pltpu.make_async_copy(ref, ref, rs_rcv.at[c, way, step])

    def first(c):
        pltpu.make_async_copy(recv.at[c], recv.at[c], d_rcv.at[c]).wait()
        gate = up = back = None
        for b in range(2):
            both = recv[c, b].astype(F32)
            x = both[:, :SL].reshape(rows, feat).astype(BF16)
            g = both[:, SL:].reshape(rows, feat).astype(BF16)
            xs[b, c * rows : (c + 1) * rows] = x
            gs[b, c * rows : (c + 1) * rows] = g
        x = jnp.concatenate([xs[0, c * rows : (c + 1) * rows], xs[1, c * rows : (c + 1) * rows]], axis=1)
        for h in range(2):
            cols = slice(h * hh, (h + 1) * hh)
            gate = dot(x, wg[:, cols]).astype(BF16).reshape(n_z, zr, hh)
            up = dot(x, wu[:, cols]).astype(BF16).reshape(n_z, zr, hh)
            back = dot(gs[0, c * rows : (c + 1) * rows], wd[0, cols], COLS)
            back = back + dot(gs[1, c * rows : (c + 1) * rows], wd[1, cols], COLS)
            back = back.astype(BF16).reshape(n_z, zr, hh)
            part[c, :, h, 0:zr] = gate
            part[c, :, h, zr : 2 * zr] = up
            part[c, :, h, 2 * zr : 3 * zr] = back
        for way in range(2):
            rs_copy(c, way, 0).start()

    def rs_hop(c, step):
        for way in range(2):
            rs_landed(c, way, step - 1).wait()
            k = half - step
            d = lax.rem(z + k, n_z) if way == 0 else lax.rem(z + n_z - k, n_z)
            if step == 1:
                part[c, d, way] = (part[c, d, way].astype(F32) + rsr[c, way, 0, way].astype(F32)).astype(BF16)
            else:
                part[c, d] = (part[c, d].astype(F32) + rsr[c, way, step - 1].astype(F32)).astype(BF16)
            rs_copy(c, way, step).start()

    def middle(c):
        for way in range(2):
            rs_landed(c, way, half - 1).wait()
        total = part[c, z].astype(F32) + rsr[c, 0, half - 1].astype(F32) + rsr[c, 1, half - 1].astype(F32)
        gate, up, back = total[:, 0:zr], total[:, zr : 2 * zr], total[:, 2 * zr :]
        sig = jax.nn.sigmoid(gate)
        act = gate * sig
        hidden = act * up
        grad_pre = back * up * sig * (1.0 + gate * (1.0 - sig))
        grad_up = back * act
        ag[c, z, :, 0:zr] = hidden.astype(BF16)
        ag[c, z, :, zr : 2 * zr] = grad_pre.astype(BF16)
        ag[c, z, :, 2 * zr : 3 * zr] = grad_up.astype(BF16)
        for way in range(2):
            ag_copy(c, way, 0).start()

    def ag_hop(c, step):
        for way in range(2):
            ag_landed(c, way, step - 1).wait()
            ag_copy(c, way, step).start()

    def piece(c, i, h):
        return ag[c, :, h, i * zr : (i + 1) * zr].reshape(rows, hh)

    def last(c):
        for way in range(2):
            ag_landed(c, way, half - 1).wait()
        for b in range(2):
            out = back = None
            for h in range(2):
                cols = slice(h * hh, (h + 1) * hh)
                fs = slice(b * feat, (b + 1) * feat)
                o = dot(piece(c, 0, h), wd[b, cols])
                r = dot(piece(c, 1, h), wg[fs, cols], COLS) + dot(piece(c, 2, h), wu[fs, cols], COLS)
                out = o if out is None else out + o
                back = r if back is None else back + r
            outb[c, b] = jnp.concatenate(
                [out.reshape(n_src, SL, feat), back.reshape(n_src, SL, feat)], axis=1
            ).astype(BF16)

        @pl.loop(0, n_exp)
        def _(t):
            i = lax.rem(me // 2 + t // 2 + 1, n_src)
            b = lax.rem(t, 2)
            j = 2 * i + core
            there = jnp.logical_or(j != me, b != core)

            @pl.when(there)
            def _():
                pltpu.make_async_remote_copy(
                    src_ref=outb.at[c, b, i], dst_ref=cbuf.at[c, me],
                    send_sem=c_snd.at[c], recv_sem=c_rcv.at[c],
                    device_id=dev(j, z, b), device_id_type=MESH,
                ).start()

            @pl.when(jnp.logical_not(there))
            def _():
                pltpu.make_async_copy(outb.at[c, b, i], cbuf.at[c, me], c_rcv.at[c]).start()
                pltpu.make_async_copy(outb.at[c, b, i], trash.at[1, c], c_snd.at[c]).start()

    stages = [first]
    for s in range(1, half):
        stages.append(functools.partial(rs_hop, step=s))
    stages.append(middle)
    for s in range(1, half):
        stages.append(functools.partial(ag_hop, step=s))
    stages.append(last)
    skew = 1
    for t in range(len(stages) + skew * (CH - 1)):
        for c in range(CH):
            s = t - skew * c
            if 0 <= s < len(stages):
                stages[s](c)

    def all_of(i, h):
        return jnp.concatenate([piece(c, i, h) for c in range(CH)], axis=0)

    for h in range(2):
        cols = slice(h * hh, (h + 1) * hh)
        gsend[0, :, cols] = dot(xs[1 - core], all_of(1, h), ROWS).astype(BF16)
        gsend[1, :, cols] = dot(xs[1 - core], all_of(2, h), ROWS).astype(BF16)
        gdsend[cols] = dot(all_of(0, h), gs[1 - core], ROWS).astype(BF16)

    def grad_copy(i):
        src, dst = ((gsend, grecv), (gdsend, gdrecv))[i]
        return pltpu.make_async_remote_copy(
            src_ref=src, dst_ref=dst, send_sem=g_snd.at[i], recv_sem=g_rcv.at[i],
            device_id=dev(me, z, 1 - core), device_id_type=MESH,
        )

    for i in range(2):
        grad_copy(i).start()
    for h in range(2):
        cols = slice(h * hh, (h + 1) * hh)
        gacc[0, :, cols] = dot(xs[core], all_of(1, h), ROWS)
        gacc[1, :, cols] = dot(xs[core], all_of(2, h), ROWS)
        gdacc[cols] = dot(all_of(0, h), gs[core], ROWS)

    for i in range(2):
        grad_copy(i).wait_recv()
    ggate[0] = (gacc[0] + grecv[0].astype(F32)).astype(BF16)
    gup[0] = (gacc[1] + grecv[1].astype(F32)).astype(BF16)
    gdown[0] = (gdacc[...] + gdrecv[...].astype(F32)).astype(BF16)

    mix = grad = None
    for c in range(CH):
        pltpu.make_async_copy(cbuf.at[c], cbuf.at[c], c_rcv.at[c]).wait()
        got = cbuf[c].reshape(wide, feat)
        m = dot(wmat[c, 0], got) + dot(wmat[c, 1], got)
        g = dot(wmat[c, 2], got)
        mix = m if mix is None else mix + m
        grad = g if grad is None else grad + g
    mixed[...] = mix.astype(BF16)
    gtok[...] = grad.astype(BF16)

    for i in range(3):
        weight_copy(i).wait_send()
    for i in range(2):
        grad_copy(i).wait_send()
    for c in range(CH):
        pltpu.make_async_copy(send.at[c], send.at[c], d_snd.at[c]).wait()
        pltpu.make_async_copy(outb.at[c], outb.at[c], c_snd.at[c]).wait()
        for way in range(2):
            for s in range(half):
                rs_copy(c, way, s).wait_send()
                ag_copy(c, way, s).wait_send()


def local(tokens, cotangent, route, prob, quota, w_gate, w_up, w_down):
    n_exp = lax.axis_size("expert")
    n_z = lax.axis_size("dp") // 2
    tok_n, feat = tokens.shape
    hid = w_gate.shape[2]
    half = n_z // 2
    n_src = n_exp // 2
    rows = n_src * SL
    zr = rows // n_z
    hh = hid // 2
    vm = pl.BlockSpec(memory_space=pltpu.VMEM)
    hbm = pl.BlockSpec(memory_space=pl.ANY)
    sm = pl.BlockSpec(memory_space=pltpu.SMEM)
    dma = pltpu.SemaphoreType.DMA
    return pl.pallas_call(
        functools.partial(kernel, n_exp, n_z),
        out_shape=(
            jax.ShapeDtypeStruct((tok_n, feat), BF16),
            jax.ShapeDtypeStruct((tok_n, feat), BF16),
            jax.ShapeDtypeStruct((1, feat, hid), BF16),
            jax.ShapeDtypeStruct((1, feat, hid), BF16),
            jax.ShapeDtypeStruct((1, hid, feat), BF16),
        ),
        in_specs=[vm, vm, vm, vm, sm, hbm, hbm, hbm],
        out_specs=[vm] * 5,
        scratch_shapes=[
            pltpu.VMEM((2 * feat, hid), BF16),
            pltpu.VMEM((2 * feat, hid), BF16),
            pltpu.VMEM((2, hid, feat), BF16),
            pltpu.VMEM((CH, n_exp, 2 * SL, feat), BF16),
            pltpu.VMEM((CH, 2, n_src, 2 * SL, feat), BF16),
            pltpu.VMEM((2, CH, 2 * SL, feat), BF16),
            pltpu.VMEM((2, CH * rows, feat), BF16),
            pltpu.VMEM((2, CH * rows, feat), BF16),
            pltpu.VMEM((CH, n_z, 2, 3 * zr, hh), BF16),
            pltpu.VMEM((CH, 2, half, 2, 3 * zr, hh), BF16),
            pltpu.VMEM((CH, n_z, 2, 3 * zr, hh), BF16),
            pltpu.VMEM((CH, 2, n_src, 2 * SL, feat), BF16),
            pltpu.VMEM((CH, n_exp, 2 * SL, feat), BF16),
            pltpu.VMEM((CH, 3, tok_n, n_exp * 2 * SL), BF16),
            pltpu.VMEM((2, feat, hid), F32),
            pltpu.VMEM((hid, feat), F32),
            pltpu.VMEM((2, feat, hid), BF16),
            pltpu.VMEM((hid, feat), BF16),
            pltpu.VMEM((2, feat, hid), BF16),
            pltpu.VMEM((hid, feat), BF16),
            dma((3,)), dma((3,)), dma((3,)),
            dma((CH,)), dma((CH,)),
            dma((CH, 2, half)), dma((CH, 2, half)),
            dma((CH, 2, half)), dma((CH, 2, half)),
            dma((CH,)), dma((CH,)),
            dma((2,)), dma((2,)),
        ],
        compiler_params=pltpu.CompilerParams(
            collective_id=0, has_side_effects=True, vmem_limit_bytes=56 * 1024 * 1024
        ),
    )(tokens, cotangent, route, prob, quota, w_gate, w_up, w_down)


def solution(mesh):
    placed = (
        P("expert", "dp"),
        P("expert", "dp"),
        P("expert", None),
        P("expert", None),
        P(),
        P("expert", "dp", None),
        P("expert", "dp", None),
        P("expert", None, "dp"),
    )
    return jax.shard_map(
        local,
        mesh=mesh,
        in_specs=placed,
        out_specs=(
            P("expert", "dp"),
            P("expert", "dp"),
            P("expert", "dp", None),
            P("expert", "dp", None),
            P("expert", None, "dp"),
        ),
        check_vma=False,
    )
```

time: 255 us -> 105 us (0.41)
  the two profiles are of different devices: /device:TPU:8 before, /device:TPU:17 now
where the time goes in v1:
time: 105 us
  Pallas kernels  96 us (91%)
  local copies, waits for them, and re-layouts  8.1 us (8%)
    pallas_call x1, Pallas kernels, local(): pl.pallas_call(functools.partial(kernel, n_exp, n_z), out_shape=(jax.Shap...  96 us
    unnamed x17, local copies, waits for them, and re-layouts  8.1 us

profile of v1, /device:TPU:17, one launch (start us, length us, event | category | flops | bytes accessed | tf_op | source)
XLA Modules:
  0.0 104.8 jit_solution(2367986243774368015)
XLA Ops:
  0.6 0.0 copy-start.4
  0.6 1.6 %copy.13.route = s32[512,8]{1,0:T(8,128)} copy(s32[512,8]{0,1:T(8,128)} %param.10) | data formatting | bytes 32768 | tf_op args[2]
  2.2 0.0 copy-done.4
  2.2 0.8 copy.14.prob
  3.0 96.0 %shard_map.119 = (bf16[512,256]{1,0:T(8,128)(2,1)}, bf16[512,256]{1,0:T(8,128)(2,1)}, bf16[1,256,1024]{2,1,0:T(8,128)(2,1)}, bf16[1,256,1024]{2,1,0:T(8,128)(2,1)}, bf16[1,1024,256]{2,1,0:T(8,128)(2,1)}) custom-call(bf16[512,256]{1,0:T(8,128)(2,1)} %tokens.1, bf16[512,256]{1,0:T(8,128)(2,1)} %cot.1, s32[512,8]{1,0:T(8,128)} %copy.13.route, ...), custom_call_target="tpu_custom_call" | custom-call | tf_op jit(solution)/shard_map/pallas_call | solution.py:390
  99.0 0.0 copy-start.3
  99.1 0.0 copy-start.2
  99.1 1.7 %copy.20 = bf16[512,256]{1,0:T(8,128)(2,1)} copy(bf16[512,256]{1,0:T(8,128)(2,1)} %get-tuple-element.10) | data formatting | bytes 524288
  100.8 0.0 copy-done.3
  100.8 0.7 copy.21
  101.5 0.0 copy-done.2
  101.5 0.0 copy-start.1
  101.5 0.8 copy.22
  102.3 0.4 copy-done.1
  102.7 0.0 copy-start
  102.7 0.8 copy.23
  103.5 0.4 copy-done
  104.0 0.8 copy.24
Async XLA Ops:
  0.6 1.6 %copy-start.4 = (f32[512,8]{0,1:T(8,128)S(1)}, f32[512,8]{0,1:T(8,128)}, u32[]{:S(2)}) copy-start(f32[512,8]{0,1:T(8,128)} %param.11) | copy-start | bytes 49156
  99.0 1.8 %copy-start.3 = (bf16[512,256]{1,0:T(8,128)(2,1)S(1)}, bf16[512,256]{1,0:T(8,128)(2,1)}, u32[]{:S(2)}) copy-start(bf16[512,256]{1,0:T(8,128)(2,1)} %get-tuple-element.11) | copy-start | bytes 786436
  99.1 2.5 %copy-start.2 = (bf16[1,256,1024]{2,1,0:T(8,128)(2,1)S(1)}, bf16[1,256,1024]{2,1,0:T(8,128)(2,1)}, u32[]{:S(2)}) copy-start(bf16[1,256,1024]{2,1,0:T(8,128)(2,1)} %get-tuple-element.12) | copy-start | bytes 1572868
  101.5 1.2 %copy-start.1 = (bf16[1,256,1024]{2,1,0:T(8,128)(2,1)S(1)}, bf16[1,256,1024]{2,1,0:T(8,128)(2,1)}, u32[]{:S(2)}) copy-start(bf16[1,256,1024]{2,1,0:T(8,128)(2,1)} %get-tuple-element.13) | copy-start | bytes 1572868
  102.7 1.2 %copy-start = (bf16[1,1024,256]{2,1,0:T(8,128)(2,1)S(1)}, bf16[1,1024,256]{2,1,0:T(8,128)(2,1)}, u32[]{:S(2)}) copy-start(bf16[1,1024,256]{2,1,0:T(8,128)(2,1)} %get-tuple-element.14) | copy-start | bytes 1572868

commit v2 on v1

v2 whole, which is shorter than its diff:
```python
import functools

import jax
import jax.numpy as jnp
from jax import lax
from jax.experimental import pallas as pl
from jax.experimental.pallas import tpu as pltpu
from jax.sharding import PartitionSpec as P

QHI = 24
CH = 3
SL = QHI // CH
MESH = pl.DeviceIdType.MESH
F32 = jnp.float32
BF16 = jnp.bfloat16
ROWS = (((0,), (0,)), ((), ()))
COLS = (((1,), (1,)), ((), ()))


def dot(a, b, dims=(((1,), (0,)), ((), ()))):
    return lax.dot_general(a, b, dims, preferred_element_type=F32)


ARRIVE, BUSY, FLIGHT = 6.5, 2.0, 2.0


def stage_order(count):
    ready, stage, link, order = [ARRIVE * (c + 1) for c in range(CH)], [0] * CH, 0.0, []
    while len(order) < CH * count:
        c = min((c for c in range(CH) if stage[c] < count), key=lambda c: (ready[c], c))
        order.append((c, stage[c]))
        link = max(link, ready[c]) + BUSY
        ready[c] = link + FLIGHT
        stage[c] += 1
    return order


def kernel(
    n_exp, n_z,
    tok_in, cot_in, route, prob, quota, wg_in, wu_in, wd_in,
    mixed, gtok, ggate, gup, gdown,
    tokens, cot,
    wg, wu, wd, send, recv, trash, xs, gs, part, rsr, ag, outb, cbuf,
    wmat, mixacc, gacc, gdacc, agx, xsx, gsx,
    t_loc, w_loc, w_snd, w_rcv, d_snd, d_rcv, rs_snd, rs_rcv, ag_snd, ag_rcv,
    c_snd, c_rcv, x_snd, x_rcv, m_snd, m_rcv,
):
    dp = lax.axis_index("dp")
    me = lax.axis_index("expert")
    z = dp // 2
    core = lax.rem(dp, 2)
    par = lax.rem(me, 2)
    n_src = n_exp // 2
    half = n_z // 2
    tok_n, feat = tokens.shape
    hid = wg.shape[1]
    hh = hid // 2
    rows = n_src * SL
    zr = rows // n_z
    per = zr // SL
    lanes = 128

    def dev(e, zz, cc):
        return {"expert": e, "dp": zz * 2 + cc}

    right, left = lax.rem(z + 1, n_z), lax.rem(z + n_z - 1, n_z)

    loads = [
        pltpu.make_async_copy(tok_in, tokens, t_loc.at[0]),
        pltpu.make_async_copy(cot_in, cot, t_loc.at[1]),
    ]
    for copy in loads:
        copy.start()

    barrier = pltpu.get_barrier_semaphore()

    def greet(e, zz, cc):
        pl.semaphore_signal(barrier, inc=1, device_id=dev(e, zz, cc), device_id_type=MESH)

    greet(me, right, core)
    greet(me, left, core)

    @pl.loop(1, n_exp)
    def _(t):
        greet(lax.rem(me + t, n_exp), z, par)

    @pl.when(core != par)
    def _():
        greet(me, z, par)

    @pl.loop(0, n_src)
    def _(t):
        greet(2 * t + core, z, 1 - par)

    own = [
        pltpu.make_async_copy(wg_in.at[0], wg.at[pl.ds(core * feat, feat)], w_loc.at[0]),
        pltpu.make_async_copy(wu_in.at[0], wu.at[pl.ds(core * feat, feat)], w_loc.at[1]),
        pltpu.make_async_copy(wd_in.at[0], wd.at[core], w_loc.at[2]),
    ]
    for copy in own:
        copy.start()

    mine = lax.broadcasted_iota(jnp.int32, (n_exp, tok_n), 0)
    match = jnp.zeros((n_exp, tok_n), F32)
    pe_t = jnp.zeros((n_exp, tok_n), F32)
    for k in range(route.shape[0]):
        hit = route[k : k + 1] == mine
        match = jnp.where(hit, 1.0, match)
        pe_t = jnp.where(hit, prob[k : k + 1], pe_t)
    earlier = lax.broadcasted_iota(jnp.int32, (tok_n, tok_n), 0) < lax.broadcasted_iota(
        jnp.int32, (tok_n, tok_n), 1
    )
    before = dot(match.astype(BF16), earlier.astype(F32).astype(BF16))
    row1 = lax.broadcasted_iota(jnp.int32, (n_exp, 1), 0)
    quotas = jnp.zeros((n_exp, 1), jnp.int32)
    for e in range(n_exp):
        quotas = jnp.where(row1 == e, quota[e], quotas)
    eff_t = jnp.where((match > 0.0) & (before < quotas.astype(F32)), before, 255.0)
    for copy in loads:
        copy.wait()

    others = par == core
    pl.semaphore_wait(barrier, n_exp + n_src + 2 - others.astype(jnp.int32))

    shared = [
        (wg_in.at[0], wg.at[pl.ds(core * feat, feat)]),
        (wu_in.at[0], wu.at[pl.ds(core * feat, feat)]),
        (wd_in.at[0], wd.at[core]),
    ]

    def weight_copy(i):
        return pltpu.make_async_remote_copy(
            src_ref=shared[i][0], dst_ref=shared[i][1], send_sem=w_snd.at[i], recv_sem=w_rcv.at[i],
            device_id=dev(me, z, 1 - core), device_id_type=MESH,
        )

    slot = lax.broadcasted_iota(jnp.int32, (n_exp, SL, tok_n), 1).astype(F32)
    for c in range(CH):
        hit = eff_t[:, None, :] == slot + float(c * SL)
        pick = jnp.where(hit, 1.0, 0.0).reshape(n_exp * SL, tok_n)
        weight = jnp.where(hit, pe_t[:, None, :], 0.0).reshape(n_exp * SL, tok_n)
        slot_prob = jnp.sum(weight, axis=1, keepdims=True)
        pick = pick.astype(BF16)
        picked = dot(pick, tokens[...]).reshape(n_exp, SL, feat)
        grads = (dot(pick, cot[...]) * slot_prob).reshape(n_exp, SL, feat)
        send[c] = jnp.concatenate([picked, grads], axis=1).astype(BF16)

        def to_expert(e):
            return pltpu.make_async_remote_copy(
                src_ref=send.at[c, e], dst_ref=recv.at[c, core, me // 2],
                send_sem=d_snd.at[c], recv_sem=d_rcv.at[c],
                device_id=dev(e, z, par), device_id_type=MESH,
            )

        @pl.loop(1, n_exp)
        def _(t):
            to_expert(lax.rem(me + t, n_exp)).start()

        @pl.when(core != par)
        def _():
            to_expert(me).start()

        @pl.when(core == par)
        def _():
            pltpu.make_async_copy(send.at[c, me], recv.at[c, core, me // 2], d_rcv.at[c]).start()
            pltpu.make_async_copy(send.at[c, me], trash.at[0, c], d_snd.at[c]).start()

        if c == 0:
            for i in range(3):
                weight_copy(i).start()

    for copy in own:
        copy.wait()
    for i in range(3):
        weight_copy(i).wait_recv()

    wide = n_exp * 2 * SL

    def tables(c):
        fill = jnp.zeros((lanes - n_exp, tok_n), F32)
        eff = jnp.concatenate([eff_t, fill], axis=0).T.astype(BF16)
        pe = jnp.concatenate([pe_t, fill], axis=0).T
        spread = (
            lax.broadcasted_iota(jnp.int32, (lanes, wide), 1) // (2 * SL)
            == lax.broadcasted_iota(jnp.int32, (lanes, wide), 0)
        ).astype(F32).astype(BF16)
        pe_hi = pe.astype(BF16)
        pe_lo = (pe - pe_hi.astype(F32)).astype(BF16)
        eff_x = dot(eff, spread)
        place = lax.rem(lax.broadcasted_iota(jnp.int32, (tok_n, wide), 1), 2 * SL)
        hit = eff_x == (lax.rem(place, SL) + c * SL).astype(F32)
        out_hit = hit & (place < SL)
        wmat[c, 0] = jnp.where(out_hit, dot(pe_hi, spread), 0.0).astype(BF16)
        wmat[c, 1] = jnp.where(out_hit, dot(pe_lo, spread), 0.0).astype(BF16)
        wmat[c, 2] = jnp.where(hit & (place >= SL), 1.0, 0.0).astype(BF16)

    def away(way, k):
        return lax.rem(z + k, n_z) if way == 0 else lax.rem(z + n_z - k, n_z)

    def longest(h, way):
        return half if way == h else half - 1

    def rs_copy(c, h, way, k):
        return pltpu.make_async_remote_copy(
            src_ref=part.at[c, away(way, k), h], dst_ref=rsr.at[c, h, way, k - 1],
            send_sem=rs_snd.at[c, h, way, k - 1], recv_sem=rs_rcv.at[c, h, way, k - 1],
            device_id=dev(me, (right, left)[way], core), device_id_type=MESH,
        )

    def rs_landed(c, h, way, k):
        ref = rsr.at[c, h, way, k - 1]
        return pltpu.make_async_copy(ref, ref, rs_rcv.at[c, h, way, k - 1])

    def ag_copy(c, h, way, k):
        ref = ag.at[c, away(1 - way, k), h]
        return pltpu.make_async_remote_copy(
            src_ref=ref, dst_ref=ref, send_sem=ag_snd.at[c, h, way, k], recv_sem=ag_rcv.at[c, h, way, k],
            device_id=dev(me, (right, left)[way], core), device_id_type=MESH,
        )

    def ag_landed(c, h, way, k):
        ref = ag.at[c, away(1 - way, k + 1), h]
        return pltpu.make_async_copy(ref, ref, ag_rcv.at[c, h, way, k])

    def first(c):
        pltpu.make_async_copy(recv.at[c], recv.at[c], d_rcv.at[c]).wait()
        gate = up = back = None
        for b in range(2):
            both = recv[c, b].astype(F32)
            x = both[:, :SL].reshape(rows, feat).astype(BF16)
            g = both[:, SL:].reshape(rows, feat).astype(BF16)
            xs[b, c * rows : (c + 1) * rows] = x
            gs[b, c * rows : (c + 1) * rows] = g
        x = jnp.concatenate([xs[0, c * rows : (c + 1) * rows], xs[1, c * rows : (c + 1) * rows]], axis=1)
        for h in range(2):
            cols = slice(h * hh, (h + 1) * hh)
            gate = dot(x, wg[:, cols]).astype(BF16).reshape(n_z, zr, hh)
            up = dot(x, wu[:, cols]).astype(BF16).reshape(n_z, zr, hh)
            back = dot(gs[0, c * rows : (c + 1) * rows], wd[0, cols], COLS)
            back = back + dot(gs[1, c * rows : (c + 1) * rows], wd[1, cols], COLS)
            back = back.astype(BF16).reshape(n_z, zr, hh)
            part[c, :, h, 0:zr] = gate
            part[c, :, h, zr : 2 * zr] = up
            part[c, :, h, 2 * zr : 3 * zr] = back
        for h in range(2):
            for way in (h, 1 - h):
                rs_copy(c, h, way, longest(h, way)).start()

        for i in range(2):
            x_copy(c, i).start()

    def to_sibling(src, dst, snd, rcv):
        return pltpu.make_async_remote_copy(
            src_ref=src, dst_ref=dst, send_sem=snd, recv_sem=rcv,
            device_id=dev(me, z, 1 - core), device_id_type=MESH,
        )

    def x_copy(c, i):
        src, dst = ((xs, xsx), (gs, gsx))[i]
        part_rows = pl.ds(c * rows, rows)
        return to_sibling(src.at[1 - core, part_rows], dst.at[part_rows], x_snd.at[c, i], x_rcv.at[c, i])

    def block_at(p):
        return away(p % 2, (p + 1) // 2)

    def m_copy(c, p):
        d = block_at(p)
        return to_sibling(ag.at[c, d], agx.at[c, d], m_snd.at[c, p], m_rcv.at[c, p])

    def rs_hop(c, step):
        for h in range(2):
            for way in (h, 1 - h):
                k = longest(h, way) - step
                if k >= 1:
                    rs_landed(c, h, way, k + 1).wait()
                    d = away(way, k)
                    part[c, d, h] = (part[c, d, h].astype(F32) + rsr[c, h, way, k].astype(F32)).astype(BF16)
                    rs_copy(c, h, way, k).start()

    def middle(c):
        for h in range(2):
            for way in (1 - h, h):
                rs_landed(c, h, way, 1).wait()
            total = part[c, z, h].astype(F32) + rsr[c, h, 0, 0].astype(F32) + rsr[c, h, 1, 0].astype(F32)
            gate, up, back = total[0:zr], total[zr : 2 * zr], total[2 * zr :]
            sig = jax.nn.sigmoid(gate)
            act = gate * sig
            ag[c, z, h, 0:zr] = (act * up).astype(BF16)
            ag[c, z, h, zr : 2 * zr] = (back * up * sig * (1.0 + gate * (1.0 - sig))).astype(BF16)
            ag[c, z, h, 2 * zr : 3 * zr] = (back * act).astype(BF16)
            for way in (h, 1 - h):
                ag_copy(c, h, way, 0).start()
        stream(c, [0])

    def ag_hop(c, step):
        for h in range(2):
            for way in (h, 1 - h):
                if step < longest(h, way):
                    ag_landed(c, h, way, step - 1).wait()
                    ag_copy(c, h, way, step).start()
                else:
                    ag_landed(c, h, way, step - 1).wait()
        stream(c, [2 * step - 1, 2 * step])

    def piece(c, i, h, held=ag):
        return held[c, :, h, i * zr : (i + 1) * zr].reshape(rows, hh)

    def to_token(c, i, b):
        return pltpu.make_async_remote_copy(
            src_ref=outb.at[c, b, i], dst_ref=cbuf.at[c, me],
            send_sem=c_snd.at[c], recv_sem=c_rcv.at[c],
            device_id=dev(2 * i + core, z, b), device_id_type=MESH,
        )

    def to_self(c):
        pltpu.make_async_copy(outb.at[c, core, me // 2], cbuf.at[c, me], c_rcv.at[c]).start()
        pltpu.make_async_copy(outb.at[c, core, me // 2], trash.at[1, c], c_snd.at[c]).start()

    def products(get, b):
        out = back = None
        for h in range(2):
            cols = slice(h * hh, (h + 1) * hh)
            fs = slice(b * feat, (b + 1) * feat)
            o = dot(get(0, h), wd[b, cols])
            r = dot(get(1, h), wg[fs, cols], COLS) + dot(get(2, h), wu[fs, cols], COLS)
            out = o if out is None else out + o
            back = r if back is None else back + r
        both = [v.reshape(v.shape[0] // SL, SL, feat) for v in (out, back)]
        return jnp.concatenate(both, axis=1).astype(BF16)

    def stream(c, places):
        ds = [block_at(p) for p in places]
        for p in places:
            m_copy(c, p).start()

        def get(i, h):
            return jnp.concatenate([ag[c, d, h, i * zr : (i + 1) * zr] for d in ds], axis=0)

        for b in range(2):
            both = products(get, b)
            for q, d in enumerate(ds):
                for r in range(per):
                    outb[c, b, d * per + r] = both[q * per + r]
        for d in ds:
            for r in range(per):
                i = d * per + r
                mine_too = (par == core) & (i == me // 2)
                for b in range(2):
                    here = mine_too & (core == b)

                    @pl.when(jnp.logical_not(here))
                    def _():
                        to_token(c, i, b).start()

                    @pl.when(here)
                    def _():
                        to_self(c)

    def last(c):
        for h in range(2):
            ag_landed(c, h, h, half - 1).wait()
        stream(c, [n_z - 1])

    def weight_grads(c):
        for i in range(2):
            x_copy(c, i).wait_recv()
        for p in range(n_z):
            m_copy(c, p).wait_recv()
        part_rows = slice(c * rows, (c + 1) * rows)
        x = jnp.concatenate([xs[core, part_rows], xsx[part_rows]], axis=0)
        g = jnp.concatenate([gs[core, part_rows], gsx[part_rows]], axis=0)
        for h in range(2):
            cols = slice(h * hh, (h + 1) * hh)
            hidden, pre, up = (
                jnp.concatenate([piece(c, i, h), piece(c, i, h, agx)], axis=0) for i in range(3)
            )
            sums = [dot(x, pre, ROWS), dot(x, up, ROWS), dot(hidden, g, ROWS)]
            refs = [gacc.at[0, :, cols], gacc.at[1, :, cols], gdacc.at[cols]]
            outs = [ggate.at[0, :, cols], gup.at[0, :, cols], gdown.at[0, cols]]
            for total, ref, out in zip(sums, refs, outs):
                if c > 0:
                    total = total + ref[...]
                if c < CH - 1:
                    ref[...] = total
                else:
                    out[...] = total.astype(BF16)

    def mix(c):
        pltpu.make_async_copy(cbuf.at[c], cbuf.at[c], c_rcv.at[c]).wait()
        got = cbuf[c].reshape(wide, feat)
        m = dot(wmat[c, 0], got) + dot(wmat[c, 1], got)
        g = dot(wmat[c, 2], got)
        if c > 0:
            m, g = m + mixacc[0], g + mixacc[1]
        if c < CH - 1:
            mixacc[0], mixacc[1] = m, g
        else:
            mixed[...], gtok[...] = m.astype(BF16), g.astype(BF16)

    stages = [first]
    for s in range(1, half):
        stages.append(functools.partial(rs_hop, step=s))
    stages.append(middle)
    for s in range(1, half):
        stages.append(functools.partial(ag_hop, step=s))
    stages.append(last)
    order = stage_order(len(stages))
    for c, stage in order:
        stages[stage](c)
        if c == 0 and 2 <= stage < 2 + CH:
            tables(stage - 2)
        if (c, stage) == (CH - 1, len(stages) - 2):
            weight_grads(0)
            mix(0)
            weight_grads(1)
    mix(1)
    weight_grads(2)
    mix(2)

    for i in range(3):
        weight_copy(i).wait_send()
    for c in range(CH):
        pltpu.make_async_copy(send.at[c], send.at[c], d_snd.at[c]).wait()
        pltpu.make_async_copy(outb.at[c], outb.at[c], c_snd.at[c]).wait()
        for i in range(2):
            x_copy(c, i).wait_send()
        for p in range(n_z):
            m_copy(c, p).wait_send()
        for h in range(2):
            for way in range(2):
                for k in range(longest(h, way)):
                    rs_copy(c, h, way, k + 1).wait_send()
                    ag_copy(c, h, way, k).wait_send()

def finish(*refs):
    ins, outs, sem = refs[:5], refs[5:10], refs[10]
    copies = [pltpu.make_async_copy(src, dst, sem.at[i]) for i, (src, dst) in enumerate(zip(ins, outs))]
    for copy in copies:
        copy.start()
    for copy in copies:
        copy.wait()


def local(tokens, cotangent, route, prob, quota, w_gate, w_up, w_down):
    n_exp = lax.axis_size("expert")
    n_z = lax.axis_size("dp") // 2
    tok_n, feat = tokens.shape
    hid = w_gate.shape[2]
    half = n_z // 2
    n_src = n_exp // 2
    rows = n_src * SL
    zr = rows // n_z
    hh = hid // 2
    vm = pl.BlockSpec(memory_space=pltpu.VMEM)
    hbm = pl.BlockSpec(memory_space=pltpu.HBM)
    sm = pl.BlockSpec(memory_space=pltpu.SMEM)
    dma = pltpu.SemaphoreType.DMA
    shapes = (
        jax.ShapeDtypeStruct((tok_n, feat), BF16),
        jax.ShapeDtypeStruct((tok_n, feat), BF16),
        jax.ShapeDtypeStruct((1, feat, hid), BF16),
        jax.ShapeDtypeStruct((1, feat, hid), BF16),
        jax.ShapeDtypeStruct((1, hid, feat), BF16),
    )
    outs = pl.pallas_call(
        functools.partial(kernel, n_exp, n_z),
        out_shape=tuple(pltpu.VMEM(s.shape, s.dtype) for s in shapes),
        in_specs=[hbm, hbm, vm, vm, sm, hbm, hbm, hbm],
        out_specs=[vm] * 5,
        scratch_shapes=[
            pltpu.VMEM((tok_n, feat), BF16),
            pltpu.VMEM((tok_n, feat), BF16),
            pltpu.VMEM((2 * feat, hid), BF16),
            pltpu.VMEM((2 * feat, hid), BF16),
            pltpu.VMEM((2, hid, feat), BF16),
            pltpu.VMEM((CH, n_exp, 2 * SL, feat), BF16),
            pltpu.VMEM((CH, 2, n_src, 2 * SL, feat), BF16),
            pltpu.VMEM((2, CH, 2 * SL, feat), BF16),
            pltpu.VMEM((2, CH * rows, feat), BF16),
            pltpu.VMEM((2, CH * rows, feat), BF16),
            pltpu.VMEM((CH, n_z, 2, 3 * zr, hh), BF16),
            pltpu.VMEM((CH, 2, 2, half, 3 * zr, hh), BF16),
            pltpu.VMEM((CH, n_z, 2, 3 * zr, hh), BF16),
            pltpu.VMEM((CH, 2, n_src, 2 * SL, feat), BF16),
            pltpu.VMEM((CH, n_exp, 2 * SL, feat), BF16),
            pltpu.VMEM((CH, 3, tok_n, n_exp * 2 * SL), BF16),
            pltpu.VMEM((2, tok_n, feat), F32),
            pltpu.VMEM((2, feat, hid), F32),
            pltpu.VMEM((hid, feat), F32),
            pltpu.VMEM((CH, n_z, 2, 3 * zr, hh), BF16),
            pltpu.VMEM((CH * rows, feat), BF16),
            pltpu.VMEM((CH * rows, feat), BF16),
            dma((2,)),
            dma((3,)), dma((3,)), dma((3,)),
            dma((CH,)), dma((CH,)),
            dma((CH, 2, 2, half)), dma((CH, 2, 2, half)),
            dma((CH, 2, 2, half)), dma((CH, 2, 2, half)),
            dma((CH,)), dma((CH,)),
            dma((CH, 2)), dma((CH, 2)),
            dma((CH, n_z)), dma((CH, n_z)),
        ],
        compiler_params=pltpu.CompilerParams(
            collective_id=0, has_side_effects=True, vmem_limit_bytes=63000 * 1024
        ),
    )(tokens, cotangent, route.T, prob.T, quota, w_gate, w_up, w_down)
    return pl.pallas_call(
        finish,
        out_shape=shapes,
        in_specs=[vm] * 5,
        out_specs=[hbm] * 5,
        scratch_shapes=[dma((5,))],
        compiler_params=pltpu.CompilerParams(vmem_limit_bytes=8 * 1024 * 1024),
    )(*outs)


def solution(mesh):
    placed = (
        P("expert", "dp"),
        P("expert", "dp"),
        P("expert", None),
        P("expert", None),
        P(),
        P("expert", "dp", None),
        P("expert", "dp", None),
        P("expert", None, "dp"),
    )
    return jax.shard_map(
        local,
        mesh=mesh,
        in_specs=placed,
        out_specs=(
            P("expert", "dp"),
            P("expert", "dp"),
            P("expert", "dp", None),
            P("expert", "dp", None),
            P("expert", None, "dp"),
        ),
        check_vma=False,
    )
```

time: 105 us -> 90.5 us (0.86)
  the two profiles are of different devices: /device:TPU:17 before, /device:TPU:33 now
where the time goes in v2:
time: 90.5 us; the launch traced here: 90.3 us
  Pallas kernels  89.5 us (99%)
    pallas_call x1, Pallas kernels, local(): pl.pallas_call(functools.partial(kernel, n_exp, n_z), out_shape=tuple((pl...  88.2 us

profile of v2, /device:TPU:33, one launch (start us, length us, event | category | flops | bytes accessed | tf_op | source)
XLA Modules:
  0.0 90.3 jit_solution(13343778449535270289)
XLA Ops:
  0.6 88.2 %shard_map.119 = (bf16[512,256]{1,0:T(8,128)(2,1)S(1)}, bf16[512,256]{1,0:T(8,128)(2,1)S(1)}, bf16[1,256,1024]{2,1,0:T(8,128)(2,1)S(1)}, bf16[1,256,1024]{2,1,0:T(8,128)(2,1)S(1)}, bf16[1,1024,256]{2,1,0:T(8,128)(2,1)S(1)}) custom-call(bf16[512,256]{1,0:T(8,128)(2,1)} %tok_in.1, bf16[512,256]{1,0:T(8,128)(2,1)} %cot_in.1, s32[8,512]{1,0:T(8,128)} %bitcast.2, ...), custom_call_target="tpu_custom_call" | custom-call | tf_op jit(solution)/shard_map/pallas_call | solution.py:465
  88.8 1.4 %shard_map.120 = (bf16[512,256]{1,0:T(8,128)(2,1)}, bf16[512,256]{1,0:T(8,128)(2,1)}, bf16[1,256,1024]{2,1,0:T(8,128)(2,1)}, bf16[1,256,1024]{2,1,0:T(8,128)(2,1)}, bf16[1,1024,256]{2,1,0:T(8,128)(2,1)}) custom-call(bf16[512,256]{1,0:T(8,128)(2,1)S(1)} %get-tuple-element.10.refs_0_, bf16[512,256]{1,0:T(8,128)(2,1)S(1)} %get-tuple-element.11.refs_1_, ...), custom_call_target="tpu_custom_call" | custom-call | tf_op jit(solution)/shard_map/pallas_call | solution.py:506

commit v3 on v2

--- a/solution.py
+++ b/solution.py
@@ -21,7 +21,7 @@
     return lax.dot_general(a, b, dims, preferred_element_type=F32)
 
 
-ARRIVE, BUSY, FLIGHT = 6.5, 2.0, 2.0
+ARRIVE, BUSY, FLIGHT, LAG = 6.5, 2.0, 2.0, 3
 
 
 def stage_order(count):
@@ -119,9 +119,6 @@
     for copy in loads:
         copy.wait()
 
-    others = par == core
-    pl.semaphore_wait(barrier, n_exp + n_src + 2 - others.astype(jnp.int32))
-
     shared = [
         (wg_in.at[0], wg.at[pl.ds(core * feat, feat)]),
         (wu_in.at[0], wu.at[pl.ds(core * feat, feat)]),
@@ -135,7 +132,8 @@
         )
 
     slot = lax.broadcasted_iota(jnp.int32, (n_exp, SL, tok_n), 1).astype(F32)
-    for c in range(CH):
+
+    def fill(c):
         hit = eff_t[:, None, :] == slot + float(c * SL)
         pick = jnp.where(hit, 1.0, 0.0).reshape(n_exp * SL, tok_n)
         weight = jnp.where(hit, pe_t[:, None, :], 0.0).reshape(n_exp * SL, tok_n)
@@ -145,6 +143,7 @@
         grads = (dot(pick, cot[...]) * slot_prob).reshape(n_exp, SL, feat)
         send[c] = jnp.concatenate([picked, grads], axis=1).astype(BF16)
 
+    def dispatch(c):
         def to_expert(e):
             return pltpu.make_async_remote_copy(
                 src_ref=send.at[c, e], dst_ref=recv.at[c, core, me // 2],
@@ -165,10 +164,15 @@
             pltpu.make_async_copy(send.at[c, me], recv.at[c, core, me // 2], d_rcv.at[c]).start()
             pltpu.make_async_copy(send.at[c, me], trash.at[0, c], d_snd.at[c]).start()
 
-        if c == 0:
-            for i in range(3):
-                weight_copy(i).start()
-
+    fill(0)
+    others = par == core
+    pl.semaphore_wait(barrier, n_exp + n_src + 2 - others.astype(jnp.int32))
+    dispatch(0)
+    for i in range(3):
+        weight_copy(i).start()
+    for c in range(1, CH):
+        fill(c)
+        dispatch(c)
     for copy in own:
         copy.wait()
     for i in range(3):
@@ -203,7 +207,7 @@
     def rs_copy(c, h, way, k):
         return pltpu.make_async_remote_copy(
             src_ref=part.at[c, away(way, k), h], dst_ref=rsr.at[c, h, way, k - 1],
-            send_sem=rs_snd.at[c, h, way, k - 1], recv_sem=rs_rcv.at[c, h, way, k - 1],
+            send_sem=rs_snd.at[c], recv_sem=rs_rcv.at[c, h, way, k - 1],
             device_id=dev(me, (right, left)[way], core), device_id_type=MESH,
         )
 
@@ -214,7 +218,7 @@
     def ag_copy(c, h, way, k):
         ref = ag.at[c, away(1 - way, k), h]
         return pltpu.make_async_remote_copy(
-            src_ref=ref, dst_ref=ref, send_sem=ag_snd.at[c, h, way, k], recv_sem=ag_rcv.at[c, h, way, k],
+            src_ref=ref, dst_ref=ref, send_sem=ag_snd.at[c], recv_sem=ag_rcv.at[c, h, way, k],
             device_id=dev(me, (right, left)[way], core), device_id_type=MESH,
         )
 
@@ -245,7 +249,6 @@
         for h in range(2):
             for way in (h, 1 - h):
                 rs_copy(c, h, way, longest(h, way)).start()
-
         for i in range(2):
             x_copy(c, i).start()
 
@@ -265,7 +268,7 @@
 
     def m_copy(c, p):
         d = block_at(p)
-        return to_sibling(ag.at[c, d], agx.at[c, d], m_snd.at[c, p], m_rcv.at[c, p])
+        return to_sibling(ag.at[c, d], agx.at[c, d], m_snd.at[c], m_rcv.at[c])
 
     def rs_hop(c, step):
         for h in range(2):
@@ -364,8 +367,7 @@
     def weight_grads(c):
         for i in range(2):
             x_copy(c, i).wait_recv()
-        for p in range(n_z):
-            m_copy(c, p).wait_recv()
+        pltpu.make_async_copy(agx.at[c], agx.at[c], m_rcv.at[c]).wait()
         part_rows = slice(c * rows, (c + 1) * rows)
         x = jnp.concatenate([xs[core, part_rows], xsx[part_rows]], axis=0)
         g = jnp.concatenate([gs[core, part_rows], gsx[part_rows]], axis=0)
@@ -385,6 +387,15 @@
                 else:
                     out[...] = total.astype(BF16)
 
+    def sent(c):
+        for ref, sem in (
+            (send.at[c], d_snd), (outb.at[c], c_snd), (ag.at[c], m_snd),
+            (part.at[c, 0 : n_z - 1], rs_snd), (ag.at[c, 0 : n_z - 1], ag_snd),
+        ):
+            pltpu.make_async_copy(ref, ref, sem.at[c]).wait()
+        for i in range(2):
+            x_copy(c, i).wait_send()
+
     def mix(c):
         pltpu.make_async_copy(cbuf.at[c], cbuf.at[c], c_rcv.at[c]).wait()
         got = cbuf[c].reshape(wide, feat)
@@ -405,32 +416,23 @@
         stages.append(functools.partial(ag_hop, step=s))
     stages.append(last)
     order = stage_order(len(stages))
-    for c, stage in order:
+    place = {(c, stage): n for n, (c, stage) in enumerate(order)}
+    after = [[] for _ in order]
+    for c in range(CH):
+        over = place[(c, len(stages) - 1)]
+        after[min(over + 1, len(order) - 1)].append(functools.partial(weight_grads, c))
+        after[min(over + LAG, len(order) - 1)].append(functools.partial(mix, c))
+        after[place[(0, 2 + c)]].append(functools.partial(tables, c))
+    for n, (c, stage) in enumerate(order):
         stages[stage](c)
-        if c == 0 and 2 <= stage < 2 + CH:
-            tables(stage - 2)
-        if (c, stage) == (CH - 1, len(stages) - 2):
-            weight_grads(0)
-            mix(0)
-            weight_grads(1)
-    mix(1)
-    weight_grads(2)
-    mix(2)
-
+        for task in after[n]:
+            task()
+
+    for c in range(CH):
+        sent(c)
     for i in range(3):
         weight_copy(i).wait_send()
-    for c in range(CH):
-        pltpu.make_async_copy(send.at[c], send.at[c], d_snd.at[c]).wait()
-        pltpu.make_async_copy(outb.at[c], outb.at[c], c_snd.at[c]).wait()
-        for i in range(2):
-            x_copy(c, i).wait_send()
-        for p in range(n_z):
-            m_copy(c, p).wait_send()
-        for h in range(2):
-            for way in range(2):
-                for k in range(longest(h, way)):
-                    rs_copy(c, h, way, k + 1).wait_send()
-                    ag_copy(c, h, way, k).wait_send()
+
 
 def finish(*refs):
     ins, outs, sem = refs[:5], refs[5:10], refs[10]
@@ -493,11 +495,11 @@
             dma((2,)),
             dma((3,)), dma((3,)), dma((3,)),
             dma((CH,)), dma((CH,)),
-            dma((CH, 2, 2, half)), dma((CH, 2, 2, half)),
-            dma((CH, 2, 2, half)), dma((CH, 2, 2, half)),
+            dma((CH,)), dma((CH, 2, 2, half)),
+            dma((CH,)), dma((CH, 2, 2, half)),
             dma((CH,)), dma((CH,)),
             dma((CH, 2)), dma((CH, 2)),
-            dma((CH, n_z)), dma((CH, n_z)),
+            dma((CH,)), dma((CH,)),
         ],
         compiler_params=pltpu.CompilerParams(
             collective_id=0, has_side_effects=True, vmem_limit_bytes=63000 * 1024

time: 90.5 us -> 88.9 us (0.982)
  the two profiles are of different devices: /device:TPU:33 before, /device:TPU:25 now
where the time goes in v3:
time: 88.9 us; the launch traced here: 88.7 us
  Pallas kernels  87.9 us (99%)
    pallas_call x1, Pallas kernels, local(): pl.pallas_call(functools.partial(kernel, n_exp, n_z), out_shape=tuple((pl...  86.6 us

profile of v3, /device:TPU:25, one launch (start us, length us, event | category | flops | bytes accessed | tf_op | source)
XLA Modules:
  0.0 88.7 jit_solution(5474138288318911175)
XLA Ops:
  0.6 86.6 %shard_map.119 = (bf16[512,256]{1,0:T(8,128)(2,1)S(1)}, bf16[512,256]{1,0:T(8,128)(2,1)S(1)}, bf16[1,256,1024]{2,1,0:T(8,128)(2,1)S(1)}, bf16[1,256,1024]{2,1,0:T(8,128)(2,1)S(1)}, bf16[1,1024,256]{2,1,0:T(8,128)(2,1)S(1)}) custom-call(bf16[512,256]{1,0:T(8,128)(2,1)} %tok_in.1, bf16[512,256]{1,0:T(8,128)(2,1)} %cot_in.1, s32[8,512]{1,0:T(8,128)} %bitcast.2, ...), custom_call_target="tpu_custom_call" | custom-call | tf_op jit(solution)/shard_map/pallas_call | solution.py:467
  87.2 1.4 %shard_map.120 = (bf16[512,256]{1,0:T(8,128)(2,1)}, bf16[512,256]{1,0:T(8,128)(2,1)}, bf16[1,256,1024]{2,1,0:T(8,128)(2,1)}, bf16[1,256,1024]{2,1,0:T(8,128)(2,1)}, bf16[1,1024,256]{2,1,0:T(8,128)(2,1)}) custom-call(bf16[512,256]{1,0:T(8,128)(2,1)S(1)} %get-tuple-element.10.refs_0_, bf16[512,256]{1,0:T(8,128)(2,1)S(1)} %get-tuple-element.11.refs_1_, ...), custom_call_target="tpu_custom_call" | custom-call | tf_op jit(solution)/shard_map/pallas_call | solution.py:508

commit v4 on v3

--- a/solution.py
+++ b/solution.py
@@ -21,7 +21,7 @@
     return lax.dot_general(a, b, dims, preferred_element_type=F32)
 
 
-ARRIVE, BUSY, FLIGHT, LAG = 6.5, 2.0, 2.0, 3
+ARRIVE, BUSY, FLIGHT, LAG = 6.5, 2.0, 2.0, 5
 
 
 def stage_order(count):
@@ -151,9 +151,12 @@
                 device_id=dev(e, z, par), device_id_type=MESH,
             )
 
-        @pl.loop(1, n_exp)
+        @pl.loop(1, n_exp // 2)
         def _(t):
             to_expert(lax.rem(me + t, n_exp)).start()
+            to_expert(lax.rem(me + n_exp - t, n_exp)).start()
+
+        to_expert(lax.rem(me + n_exp // 2, n_exp)).start()
 
         @pl.when(core != par)
         def _():
@@ -246,7 +249,6 @@
             part[c, :, h, 0:zr] = gate
             part[c, :, h, zr : 2 * zr] = up
             part[c, :, h, 2 * zr : 3 * zr] = back
-        for h in range(2):
             for way in (h, 1 - h):
                 rs_copy(c, h, way, longest(h, way)).start()
         for i in range(2):

time: 88.9 us -> 87 us (0.979)
  the two profiles are of different devices: /device:TPU:25 before, /device:TPU:33 now
where the time goes in v4:
time: 87 us; the launch traced here: 86.8 us
  Pallas kernels  86 us (99%)
    pallas_call x1, Pallas kernels, local(): pl.pallas_call(functools.partial(kernel, n_exp, n_z), out_shape=tuple((pl...  84.6 us

profile of v4, /device:TPU:33, one launch (start us, length us, event | category | flops | bytes accessed | tf_op | source)
XLA Modules:
  0.0 86.8 jit_solution(16664899765715116020)
XLA Ops:
  0.6 84.6 %shard_map.119 = (bf16[512,256]{1,0:T(8,128)(2,1)S(1)}, bf16[512,256]{1,0:T(8,128)(2,1)S(1)}, bf16[1,256,1024]{2,1,0:T(8,128)(2,1)S(1)}, bf16[1,256,1024]{2,1,0:T(8,128)(2,1)S(1)}, bf16[1,1024,256]{2,1,0:T(8,128)(2,1)S(1)}) custom-call(bf16[512,256]{1,0:T(8,128)(2,1)} %tok_in.1, bf16[512,256]{1,0:T(8,128)(2,1)} %cot_in.1, s32[8,512]{1,0:T(8,128)} %bitcast.2, ...), custom_call_target="tpu_custom_call" | custom-call | tf_op jit(solution)/shard_map/pallas_call | solution.py:469
  85.3 1.4 %shard_map.120 = (bf16[512,256]{1,0:T(8,128)(2,1)}, bf16[512,256]{1,0:T(8,128)(2,1)}, bf16[1,256,1024]{2,1,0:T(8,128)(2,1)}, bf16[1,256,1024]{2,1,0:T(8,128)(2,1)}, bf16[1,1024,256]{2,1,0:T(8,128)(2,1)}) custom-call(bf16[512,256]{1,0:T(8,128)(2,1)S(1)} %get-tuple-element.10.refs_0_, bf16[512,256]{1,0:T(8,128)(2,1)S(1)} %get-tuple-element.11.refs_1_, ...), custom_call_target="tpu_custom_call" | custom-call | tf_op jit(solution)/shard_map/pallas_call | solution.py:510

commit v5 on v4

--- a/solution.py
+++ b/solution.py
@@ -151,7 +151,7 @@
                 device_id=dev(e, z, par), device_id_type=MESH,
             )
 
-        @pl.loop(1, n_exp // 2)
+        @pl.loop(1, n_exp // 2, unroll=True)
         def _(t):
             to_expert(lax.rem(me + t, n_exp)).start()
             to_expert(lax.rem(me + n_exp - t, n_exp)).start()
@@ -426,14 +426,16 @@
         after[min(over + LAG, len(order) - 1)].append(functools.partial(mix, c))
         after[place[(0, 2 + c)]].append(functools.partial(tables, c))
     for n, (c, stage) in enumerate(order):
+        if n == len(order) - 1:
+            sent(0)
+            for i in range(3):
+                weight_copy(i).wait_send()
         stages[stage](c)
         for task in after[n]:
             task()
 
-    for c in range(CH):
+    for c in range(1, CH):
         sent(c)
-    for i in range(3):
-        weight_copy(i).wait_send()
 
 
 def finish(*refs):

time: 87 us -> 86.9 us (level)
  no operation moved by 1% of the time
where the time goes in v5:
time: 86.9 us; the launch traced here: 86.7 us
  Pallas kernels  85.9 us (99%)
    pallas_call x1, Pallas kernels, local(): pl.pallas_call(functools.partial(kernel, n_exp, n_z), out_shape=tuple((pl...  84.5 us

profile of v5, /device:TPU:33, one launch (start us, length us, event | category | flops | bytes accessed | tf_op | source)
XLA Modules:
  0.0 86.7 jit_solution(16431702401897595721)
XLA Ops:
  0.6 84.5 %shard_map.119 = (bf16[512,256]{1,0:T(8,128)(2,1)S(1)}, bf16[512,256]{1,0:T(8,128)(2,1)S(1)}, bf16[1,256,1024]{2,1,0:T(8,128)(2,1)S(1)}, bf16[1,256,1024]{2,1,0:T(8,128)(2,1)S(1)}, bf16[1,1024,256]{2,1,0:T(8,128)(2,1)S(1)}) custom-call(bf16[512,256]{1,0:T(8,128)(2,1)} %tok_in.1, bf16[512,256]{1,0:T(8,128)(2,1)} %cot_in.1, s32[8,512]{1,0:T(8,128)} %bitcast.2, ...), custom_call_target="tpu_custom_call" | custom-call | tf_op jit(solution)/shard_map/pallas_call | solution.py:471
  85.1 1.4 %shard_map.120 = (bf16[512,256]{1,0:T(8,128)(2,1)}, bf16[512,256]{1,0:T(8,128)(2,1)}, bf16[1,256,1024]{2,1,0:T(8,128)(2,1)}, bf16[1,256,1024]{2,1,0:T(8,128)(2,1)}, bf16[1,1024,256]{2,1,0:T(8,128)(2,1)}) custom-call(bf16[512,256]{1,0:T(8,128)(2,1)S(1)} %get-tuple-element.10.refs_0_, bf16[512,256]{1,0:T(8,128)(2,1)S(1)} %get-tuple-element.11.refs_1_, ...), custom_call_target="tpu_custom_call" | custom-call | tf_op jit(solution)/shard_map/pallas_call | solution.py:512
